TPU v7x, 32 devices: a whole 2x2x4 slice. The times are simulated.
32 devices in a mesh: sec: 2 (over core), dom: 16 (over z, y, x).
Axes of the slice: x: 2, y: 2, z: 4, core: 2. Of those that a mesh axis runs over, the one named last changes fastest.
Arguments:
- state: float32 [3, 8, 262144], P(None, None, ('sec', 'dom')), may hold values from -6 to 6
- send_rows: int32 [524288], P(('sec', 'dom')), may hold values from 0 to 8191, as said below
- intersection_source: int32 [524288], P(('sec', 'dom')), may hold values from 0 to 16383, as said below
- intersection_weight: float32 [524288], P(('sec', 'dom')), may hold values from 0.1 to 1
- couple_rate: float32 [2, 3], P('sec'), may hold values from 0.2 to 0.8
- atm_metric: float32 [2, 131072], P(None, 'dom'), may hold values from 0.5 to 2
- wave_speed: float32 [8], replicated, may hold values from 0.5 to 2
- ocean_adjacent: int32 [6, 131072], P(None, 'dom'), may hold values from 0 to 9215, as said below
- ocean_edges: int32 [2, 8192], P(None, 'dom'), may hold values from 0 to 8191, as said below
- ocean_kappa: float32 [131072], P('dom'), may hold values from 0.02 to 0.15
Outputs:
- new_state: float32 [3, 8, 262144], P(None, None, ('sec', 'dom'))
Inputs may be any that keep to these rules, and one draw needn't show every extreme that they name: `send_rows`: the ocean's band runs across the atmosphere's, so every block intersects every block of the other section. Within a block, cut the rows into 16 strips of 512 rows by position across the band; the 1024 slots for peer p hold the rows of strips p, p + 1, ... (modulo 16), 2 strips in all, in an order drawn from the seed; so every row fills exactly 2 slots. `intersection_source`: in each block a permutation of all 16384 received slots; the entries 2 * r .. 2 * r + 1 belong to row r. `ocean_adjacent`: each cell's neighbours on a hexagonal grid in its block's own row order; values from 8192 on name rim slots (first the cells of the previous block's last column, then those of the next block's first column, by position across the band); a cell at the band's edge names itself for a missing neighbour. `ocean_edges`: ordered by position across the band.
All inputs are finite; a program needn't handle non-finite values.
Results may differ from a plain program's by a relative error of at most 0.0001.
Values sent between devices are 32-bit elements; how exact they have to be, the bound alone decides.
A program may use at most 128 MiB of HBM per device.

v0:
```python
import jax
import jax.numpy as jnp
import numpy as np
from jax import lax
from jax.sharding import PartitionSpec as P

INTERSECTIONS = 2
TIME_STEP = 0.05


def extended_2(shard, sides, width):
    for axis, dim in sides:
        size, length = (lax.axis_size(axis), shard.shape[dim])
        up = [(i, (i + 1) % size) for i in range(size)]
        down = [(j, i) for i, j in up]
        last = lax.slice_in_dim(shard, length - width, length, axis=dim)
        leading = lax.slice_in_dim(shard, 0, width, axis=dim)
        before = lax.ppermute(last, axis, up)
        after = lax.ppermute(leading, axis, down)
        shard = jnp.concatenate([before, shard, after], axis=dim)
    return shard


def gll_derivative():
    nodes = np.array([-1.0, -1.0 / np.sqrt(5.0), 1.0 / np.sqrt(5.0), 1.0])
    barycentric = np.array(
        [
            1.0 / np.prod([nodes[first] - nodes[second] for second in range(4) if second != first])
            for first in range(4)
        ]
    )
    matrix = np.zeros((4, 4))
    for first in range(4):
        for second in range(4):
            if first != second:
                matrix[first, second] = (
                    barycentric[second] / barycentric[first] / (nodes[first] - nodes[second])
                )
        matrix[first, first] = -np.sum(matrix[first])
    return jnp.asarray(matrix, jnp.float32)


def along_first(field, derivative):
    depth, across, along = field.shape
    grouped = field.reshape(depth, across // 4, 4, along)
    return jnp.einsum(
        "ij,lejy->leiy", derivative, grouped, precision=lax.Precision.HIGHEST
    ).reshape(field.shape)


def along_second(field, derivative):
    depth, across, along = field.shape
    grouped = field.reshape(depth, across, along // 4, 4)
    return jnp.einsum(
        "ij,lxej->lxei", derivative, grouped, precision=lax.Precision.HIGHEST
    ).reshape(field.shape)


def dycore(fields, metric_x, metric_y, speeds):
    derivative = gll_derivative()
    eastward, northward, geopotential = (fields[0], fields[1], fields[2])
    slope_x = metric_x * along_first(geopotential, derivative)
    slope_y = metric_y * along_second(geopotential, derivative)
    spread = metric_x * along_first(eastward, derivative) + metric_y * along_second(
        northward, derivative
    )
    return jnp.stack(
        [
            eastward - TIME_STEP * slope_x,
            northward - TIME_STEP * slope_y,
            geopotential - TIME_STEP * speeds[:, None, None] * spread,
        ]
    )


def average_first(fields, before, after):
    phase = (jnp.arange(fields.shape[2]) % 4)[:, None]
    return jnp.where(
        phase == 3, (fields + after) * 0.5, jnp.where(phase == 0, (fields + before) * 0.5, fields)
    )


def average_second(fields):
    along = fields.shape[3]
    position = jnp.arange(along)
    phase = position % 4
    after = jnp.roll(fields, -1, axis=3)
    before = jnp.roll(fields, 1, axis=3)
    joined_after = (phase == 3) & (position < along - 1)
    joined_before = (phase == 0) & (position > 0)
    return jnp.where(
        joined_after,
        (fields + after) * 0.5,
        jnp.where(joined_before, (fields + before) * 0.5, fields),
    )


def body(
    state,
    send_rows,
    intersection_source,
    intersection_weight,
    couple_rate,
    atm_metric,
    wave_speed,
    ocean_adjacent,
    ocean_edges,
    ocean_kappa,
):
    levels = state.shape[1]
    y_points = ocean_edges.shape[1]
    x_points = state.shape[2] // y_points
    section = lax.axis_index("sec")
    atmosphere = section == 0
    surface = state[:, levels - 1]
    outgoing = surface[:, send_rows]
    slot_count = outgoing.shape[1]
    blank = jnp.zeros_like(outgoing)
    spread_out = jnp.where(
        atmosphere,
        jnp.concatenate([blank, outgoing], axis=1),
        jnp.concatenate([outgoing, blank], axis=1),
    )
    arrived = lax.all_to_all(spread_out, ("sec", "dom"), split_axis=1, concat_axis=1, tiled=True)
    incoming = lax.dynamic_slice_in_dim(arrived, (1 - section) * slot_count, slot_count, 1)
    weights = intersection_weight.reshape(-1, INTERSECTIONS)
    values = incoming[:, intersection_source].reshape(3, -1, INTERSECTIONS)
    regrid = jnp.sum(values * weights, axis=-1) / jnp.sum(weights, axis=-1)
    metric = atm_metric.reshape(2, x_points, y_points)

    def advance(current):
        grid = current.reshape(3, levels, x_points, y_points)
        return dycore(grid, metric[0], metric[1], wave_speed).reshape(current.shape)

    def unchanged(current):
        return current

    segmented = lax.cond(atmosphere, advance, unchanged, state)
    positions = jnp.arange(y_points, dtype=jnp.int32)
    left_rows = jnp.where(atmosphere, positions, ocean_edges[0])
    right_rows = jnp.where(atmosphere, (x_points - 1) * y_points + positions, ocean_edges[1])
    border = jnp.stack([segmented[:, :, left_rows], segmented[:, :, right_rows]], axis=2)
    rimmed = extended_2(border, (("dom", 2),), 1)
    western = rimmed[:, :, 0]
    eastern = rimmed[:, :, 3]

    def finish_atmosphere(operands):
        current, west_side, east_side = operands
        grid = current.reshape(3, levels, x_points, y_points)
        padded = jnp.concatenate([west_side[:, :, None], grid, east_side[:, :, None]], axis=2)
        averaged = average_second(average_first(grid, padded[:, :, :-2], padded[:, :, 2:]))
        return averaged.reshape(current.shape)

    def sweep_ocean(operands):
        current, west_side, east_side = operands
        extended = jnp.concatenate([current, west_side, east_side], axis=2)
        summed = jnp.zeros_like(current)
        for neighbor in range(6):
            summed = summed + (extended[:, :, ocean_adjacent[neighbor]] - current)
        return current + ocean_kappa * summed

    updated = lax.cond(atmosphere, finish_atmosphere, sweep_ocean, (segmented, western, eastern))
    rates = couple_rate[0][:, None]
    surface_top = updated[:, levels - 1]
    surface_top = surface_top + rates * (regrid - surface_top)
    return updated.at[:, levels - 1].set(surface_top)


def solution(mesh):
    in_specs = (
        P(None, None, ("sec", "dom")),
        P(("sec", "dom")),
        P(("sec", "dom")),
        P(("sec", "dom")),
        P("sec", None),
        P(None, "dom"),
        P(),
        P(None, "dom"),
        P(None, "dom"),
        P("dom"),
    )
    out_specs = P(None, None, ("sec", "dom"))
    return jax.shard_map(body, mesh=mesh, in_specs=in_specs, out_specs=out_specs, check_vma=False)
```

profile of v0, /device:TPU:1, one launch (start us, length us, event | category | flops | bytes accessed | tf_op | source)
XLA Modules:
  0.0 745.3 jit_solution(7190524143693755592)
XLA Ops:
  0.0 1.1 copy.204
  1.1 0.1 slice.134
  1.2 2.6 copy.190
  3.8 0.9 fusion.26
  4.7 56.6 %gather_fusion.8 = f32[16384,3]{1,0:T(8,128)} fusion(f32[3,8192]{0,1:T(8,128)} %bitcast.117, s32[16384]{0:T(1024)S(1)} %fusion.26), kind=kCustom, calls=%fused_computation.8 | custom fusion | bytes 458752 | tf_op jit(solution)/shard_map/gather | solution.py:116
  61.4 16.0 %pad_select_fusion = f32[3,32768]{0,1:T(8,128)} fusion(f32[3,16384]{0,1:T(8,128)} %bitcast.119, pred[]{:T(512)S(6)} %eq.33), kind=kLoop, calls=%fused_computation.75 | loop fusion | flops 98304 | bytes 589825 | tf_op jit(solution)/shard_map/jit(_where)/select_n | solution.py:119
  77.4 9.9 %copy.184 = f32[3,32,1024]{2,0,1:T(4,128)} copy(f32[3,32,1024]{0,2,1:T(8,128)} %bitcast.109) | data formatting | bytes 786432 | tf_op jit(solution)/shard_map/all_to_all | solution.py:124
  87.3 7.2 all-to-all-start
  94.5 0.0 copy-start.3
  94.5 0.0 copy-start.1
  94.5 0.0 copy-start
  94.5 0.0 copy-start.4
  94.5 10.6 %copy.176 = f32[3,8,8192]{1,0,2:T(4,128)} copy(f32[3,8,8192]{2,1,0:T(8,128)S(1)} %get-tuple-element.175) | data formatting | bytes 1572864 | tf_op jit(solution)/shard_map/cond | solution.py:138
  105.1 7.3 gather_fusion.7
  112.4 0.3 copy.179
  112.6 5.3 collective-permute-start.1
  117.9 7.3 gather_fusion.6
  125.2 0.3 copy.177
  125.5 0.0 collective-permute-start
  125.6 5.5 mul.165
  131.1 3.3 reduce_sum.22
  134.4 0.0 collective-permute-done.1
  134.5 482.6 %conditional.3 = (f32[3,8,8192]{2,1,0:T(8,128)}) conditional(s32[]{:T(128)} %convert_element_type.4, (f32[8192]{0:T(1024)S(1)}, f32[3,8,1,512]{3,1,2,0:T(8,128)S(1)}, f32[3,8,1,512]{3,1,2,0:T(8,128)S(1)}, f32[3,8,8192]{2,1,0:T(8,128)S(1)}, s32[6,8192]{1,0:T(8,128)S(1)}) %tuple.75, (f32[3,8,8192]{2,1,0:T(8,128)S(1)}, f32[3,8,1,512]{3,1,2,0:T(8,128)S(1)}, ...), branch_computations={%region_2.3_spmd, %region_3.4_spmd} | conditional | flops 4724864 | bytes 29720584 | solution.py:162
  134.5 0.1 pad_maximum_fusion.3
  134.5 11.9 %copy.164 = f32[3,8,9216]{1,0,2:T(4,128)} copy(f32[3,8,9216]{2,1,0:T(8,128)S(1)} %pad_maximum_fusion.3) | data formatting | bytes 1769472 | tf_op jit(solution)/shard_map/cond/branch_0_fun/concatenate | solution.py:156
  146.4 0.2 compare_select_fusion.5
  146.7 65.8 %gather_fusion = f32[8192,3,8]{2,1,0:T(4,128)} fusion(f32[3,8,9216]{1,0,2:T(4,128)} %copy.164, s32[8192]{0:T(1024)S(1)} %broadcast_clamp_fusion.5), kind=kCustom, calls=%fused_computation | custom fusion | bytes 1605632 | tf_op jit(solution)/shard_map/cond/branch_0_fun/gather | solution.py:159
  212.5 11.7 %copy.165 = f32[8192,3,8]{0,2,1:T(8,128)S(1)} copy(f32[8192,3,8]{2,1,0:T(4,128)} %gather_fusion) | data formatting | bytes 1572864 | tf_op jit(solution)/shard_map/cond/branch_0_fun/gather | solution.py:159
  224.2 65.8 %gather_fusion.1 = f32[8192,3,8]{2,1,0:T(4,128)} fusion(f32[3,8,9216]{1,0,2:T(4,128)} %copy.164, s32[8192]{0:T(1024)S(1)} %broadcast_clamp_fusion.4), kind=kCustom, calls=%fused_computation.1 | custom fusion | bytes 1605632 | tf_op jit(solution)/shard_map/cond/branch_0_fun/gather | solution.py:159
  290.0 11.7 %copy.167 = f32[8192,3,8]{0,2,1:T(8,128)S(1)} copy(f32[8192,3,8]{2,1,0:T(4,128)} %gather_fusion.1) | data formatting | bytes 1572864 | tf_op jit(solution)/shard_map/cond/branch_0_fun/gather | solution.py:159
  301.7 65.8 %gather_fusion.2 = f32[8192,3,8]{2,1,0:T(4,128)} fusion(f32[3,8,9216]{1,0,2:T(4,128)} %copy.164, s32[8192]{0:T(1024)S(1)} %broadcast_clamp_fusion.3), kind=kCustom, calls=%fused_computation.2 | custom fusion | bytes 1605632 | tf_op jit(solution)/shard_map/cond/branch_0_fun/gather | solution.py:159
  367.6 11.7 %copy.169 = f32[8192,3,8]{0,2,1:T(8,128)S(1)} copy(f32[8192,3,8]{2,1,0:T(4,128)} %gather_fusion.2) | data formatting | bytes 1572864 | tf_op jit(solution)/shard_map/cond/branch_0_fun/gather | solution.py:159
  379.2 65.8 %gather_fusion.3 = f32[8192,3,8]{2,1,0:T(4,128)} fusion(f32[3,8,9216]{1,0,2:T(4,128)} %copy.164, s32[8192]{0:T(1024)S(1)} %broadcast_clamp_fusion.2), kind=kCustom, calls=%fused_computation.3 | custom fusion | bytes 1605632 | tf_op jit(solution)/shard_map/cond/branch_0_fun/gather | solution.py:159
  445.1 12.5 %copy.171 = f32[8192,3,8]{0,2,1:T(8,128)} copy(f32[8192,3,8]{2,1,0:T(4,128)} %gather_fusion.3) | data formatting | bytes 1572864 | tf_op jit(solution)/shard_map/cond/branch_0_fun/gather | solution.py:159
  457.6 65.8 %gather_fusion.4 = f32[8192,3,8]{2,1,0:T(4,128)} fusion(f32[3,8,9216]{1,0,2:T(4,128)} %copy.164, s32[8192]{0:T(1024)S(1)} %broadcast_clamp_fusion.1), kind=kCustom, calls=%fused_computation.4 | custom fusion | bytes 1605632 | tf_op jit(solution)/shard_map/cond/branch_0_fun/gather | solution.py:159
  523.4 12.5 %copy.173 = f32[8192,3,8]{0,2,1:T(8,128)} copy(f32[8192,3,8]{2,1,0:T(4,128)} %gather_fusion.4) | data formatting | bytes 1572864 | tf_op jit(solution)/shard_map/cond/branch_0_fun/gather | solution.py:159
  535.9 65.8 %gather_fusion.5 = f32[8192,3,8]{2,1,0:T(4,128)} fusion(f32[3,8,9216]{1,0,2:T(4,128)} %copy.164, s32[8192]{0:T(1024)S(1)} %broadcast_clamp_fusion), kind=kCustom, calls=%fused_computation.5 | custom fusion | bytes 1605632 | tf_op jit(solution)/shard_map/cond/branch_0_fun/gather | solution.py:159
  601.8 12.5 %copy.175 = f32[8192,3,8]{0,2,1:T(8,128)} copy(f32[8192,3,8]{2,1,0:T(4,128)} %gather_fusion.5) | data formatting | bytes 1572864 | tf_op jit(solution)/shard_map/cond/branch_0_fun/gather | solution.py:159
  614.3 2.8 fusion.21
  617.1 1.2 slice.166
  618.3 9.2 %copy.185 = f32[3,32,1024]{0,2,1:T(8,128)} copy(f32[3,32,1024]{2,0,1:T(4,128)} %all-to-all-done) | data formatting | bytes 786432 | tf_op jit(solution)/shard_map/all_to_all | solution.py:124
  627.5 5.7 constant_dynamic-slice_fusion
  633.3 57.9 %gather_fusion.9 = f32[16384,3]{1,0:T(8,128)} fusion(f32[3,16384]{0,1:T(8,128)} %constant_dynamic-slice_fusion, s32[16384]{0:T(1024)S(1)} %fusion.27), kind=kCustom, calls=%fused_computation.9 | custom fusion | bytes 458752 | tf_op jit(solution)/shard_map/gather | solution.py:127
  691.2 48.0 %multiply_reduce_fusion = f32[3,8192]{0,1:T(8,128)} fusion(f32[3,8192,2]{0,2,1:T(2,128)} %bitcast.118, f32[8192,2]{1,0:T(8,128)} %mul.165), kind=kLoop, calls=%fused_computation.76 | loop fusion | flops 73728 | bytes 360448 | tf_op jit(solution)/shard_map/reduce_sum | solution.py:128
  739.2 2.8 copy.186
  742.0 0.1 copy_add_fusion
  742.1 0.1 copy.187
  742.2 3.0 scatter.4
  (25 shorter events, 0.1 us)
Async XLA Ops:
  61.4 33.1 %copy-start.6 = (s32[2,512]{1,0:T(2,128)S(1)}, s32[2,512]{1,0:T(2,128)}, u32[]{:S(2)}) copy-start(s32[2,512]{1,0:T(2,128)} %param.25) | copy-start | bytes 12292
  61.4 33.1 %copy-start.2 = (f32[2,8192]{1,0:T(2,128)S(1)}, f32[2,8192]{1,0:T(2,128)}, u32[]{:S(2)}) copy-start(f32[2,8192]{1,0:T(2,128)} %param.22) | copy-start | bytes 196612
  61.4 33.1 %copy-start.8 = (f32[8]{0:T(128)S(1)}, f32[8]{0:T(128)}, u32[]{:S(2)}) copy-start(f32[8]{0:T(128)} %param.23) | copy-start | bytes 100
  87.3 531.1 %all-to-all-start = ((f32[3,32,1024]{2,0,1:T(4,128)}), f32[3,32,1024]{2,0,1:T(4,128)}, u32[]{:S(2)}, u32[]{:S(2)}) async-start(f32[3,32,1024]{2,0,1:T(4,128)} %copy.184), calls=%async_computation | async-start | bytes 1048576 | tf_op jit(solution)/shard_map/all_to_all | solution.py:124
  94.5 31.0 %copy-start.3 = (s32[16384]{0:T(1024)S(1)}, s32[16384]{0:T(1024)}, u32[]{:S(2)}) copy-start(s32[16384]{0:T(1024)} %param.19) | copy-start | bytes 196612
  94.5 31.1 %copy-start.1 = (f32[16384]{0:T(1024)S(1)}, f32[16384]{0:T(1024)}, u32[]{:S(2)}) copy-start(f32[16384]{0:T(1024)} %param.20) | copy-start | bytes 196612
  94.5 39.9 %copy-start = (s32[6,8192]{1,0:T(8,128)S(1)}, s32[6,8192]{1,0:T(8,128)}, u32[]{:S(2)}) copy-start(s32[6,8192]{1,0:T(8,128)} %param.24) | copy-start | bytes 589828
  94.5 39.9 %copy-start.4 = (f32[8192]{0:T(1024)S(1)}, f32[8192]{0:T(1024)}, u32[]{:S(2)}) copy-start(f32[8192]{0:T(1024)} %param.26) | copy-start | bytes 98308
  112.6 21.8 %collective-permute-start.1 = (f32[3,8,1,512]{3,1,2,0:T(8,128)S(1)}, f32[3,8,1,512]{3,1,2,0:T(8,128)S(1)}, u32[]{:S(2)}, u32[]{:S(2)}) collective-permute-start(f32[3,8,1,512]{3,1,2,0:T(8,128)S(1)} %copy.179), channel_id=1, source_target_pairs={{1,0},{2,1},{3,2},{4,3},{5,4},{6,5},{7,6},{8,7},{9,8},{10,9},{11,1... | collective-permute-start | bytes 147464 | tf_op jit(solution)/shard_map/ppermute | solution.py:19
  125.5 9.0 %collective-permute-start = (f32[3,8,1,512]{3,1,2,0:T(8,128)S(1)}, f32[3,8,1,512]{3,1,2,0:T(8,128)S(1)}, u32[]{:S(2)}, u32[]{:S(2)}) collective-permute-start(f32[3,8,1,512]{3,1,2,0:T(8,128)S(1)} %copy.177), channel_id=1, source_target_pairs={{0,1},{1,2},{2,3},{3,4},{4,5},{5,6},{6,7},{7,8},{8,9},{9,10},{10,1... | collective-permute-start | bytes 147464 | tf_op jit(solution)/shard_map/ppermute | solution.py:18
  627.5 114.5 %copy-start.7 = (f32[1,3]{1,0:T(1,128)S(1)}, f32[1,3]{1,0:T(1,128)}, u32[]{:S(2)}) copy-start(f32[1,3]{1,0:T(1,128)} %param.21) | copy-start | bytes 40
where the time goes:
time: 748 us; the launch traced here: 745 us
  local copies, waits for them, and re-layouts  661 us (88%)
  other arithmetic  71.5 us (10%)
  starting transfers between devices  12.5 us (2%)
    gather x12, local copies, waits for them, and re-layouts, sweep_ocean(): summed = summed + (extended[:, :, ocean_adjacent[neighbor]] - current)  468 us
    gather x1, local copies, waits for them, and re-layouts, body(): values = incoming[:, intersection_source].reshape(3, -1, INTERSECTIONS)  57.9 us
    gather x1, local copies, waits for them, and re-layouts, body(): outgoing = surface[:, send_rows]  56.6 us
    reduce_sum x2, other arithmetic, body(): regrid = jnp.sum(values * weights, axis=-1) / jnp.sum(weights, axis=-1)  51.3 us
    all_to_all x2, local copies, waits for them, and re-layouts, body(): lax.all_to_all(spread_out, ('sec', 'dom'), split_axis=1, concat_axis=1, t...  19.1 us
    select_n x1, other arithmetic, body(): jnp.where(atmosphere, jnp.concatenate([blank, outgoing], axis=1), jnp.con...  16 us
  transfers between devices with their start and end apart: 3, of which 0 were waited for; matrix products, arithmetic and copies ran while one was open for 70% of the time, Pallas kernels for 0%

commit v1 on v0

--- a/solution.py
+++ b/solution.py
@@ -121,7 +121,15 @@
         jnp.concatenate([blank, outgoing], axis=1),
         jnp.concatenate([outgoing, blank], axis=1),
     )
-    arrived = lax.all_to_all(spread_out, ("sec", "dom"), split_axis=1, concat_axis=1, tiled=True)
+    arrived = jnp.concatenate(
+        lax.all_to_all(
+            jnp.stack(jnp.split(spread_out, lax.axis_size(("sec", "dom")), axis=1)),
+            ("sec", "dom"),
+            0,
+            0,
+        ),
+        axis=1,
+    )
     incoming = lax.dynamic_slice_in_dim(arrived, (1 - section) * slot_count, slot_count, 1)
     weights = intersection_weight.reshape(-1, INTERSECTIONS)
     values = incoming[:, intersection_source].reshape(3, -1, INTERSECTIONS)

time: 748 us -> 772 us (1.032)
  local copies, waits for them, and re-layouts: 661 us -> 690 us
    unnamed x18 -> x47, local copies, waits for them, and re-layouts: 3.79 us -> 29.9 us
    all_to_all x2 -> x0, local copies, waits for them, and re-layouts: 19.1 us -> none  [body(): lax.all_to_all(spread_out, ('sec', 'dom'), split_axis=1, concat_axis=1, t...]
    another operation x0 -> x2, local copies, waits for them, and re-layouts: none -> 10.7 us  [body(): jnp.stack(jnp.split(spread_out, lax.axis_size(('sec', 'dom')), axis=1))]
    reshape x0 -> x1, local copies, waits for them, and re-layouts: none -> 9.13 us  [body(): jnp.concatenate(lax.all_to_all(jnp.stack(jnp.split(spread_out, lax.axis_s...]
  transfers between devices with their start and end apart: 3 -> 3, of which waited for: 0 -> 0; matrix products, arithmetic and copies ran while one was open for 70% -> 67% of each run, Pallas kernels for 0% -> 0%
where the time goes in v1:
time: 772 us; the launch traced here: 770 us
  local copies, waits for them, and re-layouts  690 us (89%)
  other arithmetic  67.5 us (9%)
  starting transfers between devices  12.3 us (2%)
    gather x12, local copies, waits for them, and re-layouts, sweep_ocean(): summed = summed + (extended[:, :, ocean_adjacent[neighbor]] - current)  469 us
    gather x1, local copies, waits for them, and re-layouts, body(): values = incoming[:, intersection_source].reshape(3, -1, INTERSECTIONS)  58.1 us
    gather x1, local copies, waits for them, and re-layouts, body(): outgoing = surface[:, send_rows]  57 us
    reduce_sum x2, other arithmetic, body(): regrid = jnp.sum(values * weights, axis=-1) / jnp.sum(weights, axis=-1)  51.3 us
    unnamed x47, local copies, waits for them, and re-layouts  29.9 us
  transfers between devices with their start and end apart: 3, of which 0 were waited for; matrix products, arithmetic and copies ran while one was open for 67% of the time, Pallas kernels for 0%

profile of v1, /device:TPU:1, one launch (start us, length us, event | category | flops | bytes accessed | tf_op | source)
XLA Modules:
  0.0 769.9 jit_solution(2372373087660765375)
XLA Ops:
  0.0 1.1 copy.299
  1.2 2.6 copy.254
  3.9 0.9 fusion.58
  4.8 57.0 %gather_fusion.8 = f32[16384,3]{1,0:T(8,128)} fusion(f32[3,8192]{0,1:T(8,128)} %bitcast.244, s32[16384]{0:T(1024)S(1)} %get-tuple-element.175), kind=kCustom, calls=%fused_computation.8 | custom fusion | bytes 458752 | tf_op jit(solution)/shard_map/gather | solution.py:116
  61.7 12.0 %pad_select_fusion = f32[3,32768]{0,1:T(8,128)S(1)} fusion(f32[3,16384]{0,1:T(8,128)} %bitcast.246, pred[]{:T(512)S(6)} %eq.33), kind=kLoop, calls=%fused_computation.75 | loop fusion | flops 98304 | bytes 589825 | tf_op jit(solution)/shard_map/jit(_where)/select_n | solution.py:119
  73.7 0.8 fusion.57
  76.2 0.8 fusion.54
  80.4 0.8 fusion.49
  82.9 0.8 fusion.46
  86.2 0.9 fusion.42
  87.1 0.9 fusion.41
  88.8 0.8 fusion.39
  89.7 0.9 fusion.38
  90.5 0.8 fusion.37
  93.0 0.9 fusion.34
  93.9 0.9 fusion.33
  96.5 0.8 fusion.30
  98.1 0.9 fusion.28
  100.6 9.9 %copy.248 = f32[32,3,1024]{2,1,0:T(4,128)} copy(f32[32,3,1024]{1,2,0:T(8,128)} %fusion.26) | data formatting | bytes 786432 | tf_op jit(solution)/shard_map/stack | solution.py:126
  110.5 7.2 all-to-all-start
  117.9 10.6 %copy.240 = f32[3,8,8192]{1,0,2:T(4,128)} copy(f32[3,8,8192]{2,1,0:T(8,128)S(1)} %get-tuple-element.179) | data formatting | bytes 1572864 | tf_op jit(solution)/shard_map/cond | solution.py:146
  128.5 7.3 gather_fusion.7
  136.1 5.1 collective-permute-start.1
  141.2 7.3 gather_fusion.6
  148.8 5.5 mul.165
  154.3 3.3 reduce_sum.22
  157.7 483.8 %conditional.3 = (f32[3,8,8192]{2,1,0:T(8,128)}) conditional(s32[]{:T(128)} %convert_element_type.4, (f32[8192]{0:T(1024)S(1)}, f32[3,8,1,512]{3,1,2,0:T(8,128)S(1)}, f32[3,8,1,512]{3,1,2,0:T(8,128)S(1)}, f32[3,8,8192]{2,1,0:T(8,128)S(1)}, s32[6,8192]{1,0:T(8,128)S(1)}) %tuple.77, (f32[3,8,8192]{2,1,0:T(8,128)S(1)}, f32[3,8,1,512]{3,1,2,0:T(8,128)S(1)}, ...), branch_computations={%region_2.3_spmd, %region_3.4_spmd} | conditional | flops 4724864 | bytes 29720584 | solution.py:170
  157.8 11.9 %copy.228 = f32[3,8,9216]{1,0,2:T(4,128)} copy(f32[3,8,9216]{2,1,0:T(8,128)S(1)} %pad_maximum_fusion.3) | data formatting | bytes 1769472 | tf_op jit(solution)/shard_map/cond/branch_0_fun/concatenate | solution.py:164
  169.9 66.0 %gather_fusion = f32[8192,3,8]{2,1,0:T(4,128)} fusion(f32[3,8,9216]{1,0,2:T(4,128)} %copy.228, s32[8192]{0:T(1024)S(1)} %broadcast_clamp_fusion.5), kind=kCustom, calls=%fused_computation | custom fusion | bytes 1605632 | tf_op jit(solution)/shard_map/cond/branch_0_fun/gather | solution.py:167
  235.9 11.7 %copy.229 = f32[8192,3,8]{0,2,1:T(8,128)S(1)} copy(f32[8192,3,8]{2,1,0:T(4,128)} %gather_fusion) | data formatting | bytes 1572864 | tf_op jit(solution)/shard_map/cond/branch_0_fun/gather | solution.py:167
  247.6 66.0 %gather_fusion.1 = f32[8192,3,8]{2,1,0:T(4,128)} fusion(f32[3,8,9216]{1,0,2:T(4,128)} %copy.228, s32[8192]{0:T(1024)S(1)} %broadcast_clamp_fusion.4), kind=kCustom, calls=%fused_computation.1 | custom fusion | bytes 1605632 | tf_op jit(solution)/shard_map/cond/branch_0_fun/gather | solution.py:167
  313.7 11.7 %copy.231 = f32[8192,3,8]{0,2,1:T(8,128)S(1)} copy(f32[8192,3,8]{2,1,0:T(4,128)} %gather_fusion.1) | data formatting | bytes 1572864 | tf_op jit(solution)/shard_map/cond/branch_0_fun/gather | solution.py:167
  325.3 66.0 %gather_fusion.2 = f32[8192,3,8]{2,1,0:T(4,128)} fusion(f32[3,8,9216]{1,0,2:T(4,128)} %copy.228, s32[8192]{0:T(1024)S(1)} %broadcast_clamp_fusion.3), kind=kCustom, calls=%fused_computation.2 | custom fusion | bytes 1605632 | tf_op jit(solution)/shard_map/cond/branch_0_fun/gather | solution.py:167
  391.4 11.7 %copy.233 = f32[8192,3,8]{0,2,1:T(8,128)S(1)} copy(f32[8192,3,8]{2,1,0:T(4,128)} %gather_fusion.2) | data formatting | bytes 1572864 | tf_op jit(solution)/shard_map/cond/branch_0_fun/gather | solution.py:167
  403.1 66.0 %gather_fusion.3 = f32[8192,3,8]{2,1,0:T(4,128)} fusion(f32[3,8,9216]{1,0,2:T(4,128)} %copy.228, s32[8192]{0:T(1024)S(1)} %broadcast_clamp_fusion.2), kind=kCustom, calls=%fused_computation.3 | custom fusion | bytes 1605632 | tf_op jit(solution)/shard_map/cond/branch_0_fun/gather | solution.py:167
  469.1 12.5 %copy.235 = f32[8192,3,8]{0,2,1:T(8,128)} copy(f32[8192,3,8]{2,1,0:T(4,128)} %gather_fusion.3) | data formatting | bytes 1572864 | tf_op jit(solution)/shard_map/cond/branch_0_fun/gather | solution.py:167
  481.6 66.0 %gather_fusion.4 = f32[8192,3,8]{2,1,0:T(4,128)} fusion(f32[3,8,9216]{1,0,2:T(4,128)} %copy.228, s32[8192]{0:T(1024)S(1)} %broadcast_clamp_fusion.1), kind=kCustom, calls=%fused_computation.4 | custom fusion | bytes 1605632 | tf_op jit(solution)/shard_map/cond/branch_0_fun/gather | solution.py:167
  547.7 12.5 %copy.237 = f32[8192,3,8]{0,2,1:T(8,128)} copy(f32[8192,3,8]{2,1,0:T(4,128)} %gather_fusion.4) | data formatting | bytes 1572864 | tf_op jit(solution)/shard_map/cond/branch_0_fun/gather | solution.py:167
  560.2 66.0 %gather_fusion.5 = f32[8192,3,8]{2,1,0:T(4,128)} fusion(f32[3,8,9216]{1,0,2:T(4,128)} %copy.228, s32[8192]{0:T(1024)S(1)} %broadcast_clamp_fusion), kind=kCustom, calls=%fused_computation.5 | custom fusion | bytes 1605632 | tf_op jit(solution)/shard_map/cond/branch_0_fun/gather | solution.py:167
  626.2 12.5 %copy.239 = f32[8192,3,8]{0,2,1:T(8,128)} copy(f32[8192,3,8]{2,1,0:T(4,128)} %gather_fusion.5) | data formatting | bytes 1572864 | tf_op jit(solution)/shard_map/cond/branch_0_fun/gather | solution.py:167
  638.7 2.8 fusion.21
  641.5 1.2 slice.166
  642.8 9.1 %copy.249 = f32[3,32,1024]{0,2,1:T(8,128)} copy(f32[3,32,1024]{2,0,1:T(4,128)} %bitcast.67) | data formatting | bytes 786432 | tf_op jit(solution)/shard_map/reshape | solution.py:124
  651.9 5.7 constant_dynamic-slice_fusion
  657.6 58.1 %gather_fusion.9 = f32[16384,3]{1,0:T(8,128)} fusion(f32[3,16384]{0,1:T(8,128)} %constant_dynamic-slice_fusion, s32[16384]{0:T(1024)S(1)} %get-tuple-element.176), kind=kCustom, calls=%fused_computation.9 | custom fusion | bytes 458752 | tf_op jit(solution)/shard_map/gather | solution.py:135
  715.8 48.0 %multiply_reduce_fusion = f32[3,8192]{0,1:T(8,128)} fusion(f32[3,8192,2]{0,2,1:T(2,128)} %bitcast.245, f32[8192,2]{1,0:T(8,128)} %mul.165), kind=kLoop, calls=%fused_computation.76 | loop fusion | flops 73728 | bytes 360448 | tf_op jit(solution)/shard_map/reduce_sum | solution.py:136
  763.8 2.8 copy.250
  766.9 3.0 scatter.4
  (53 shorter events, 17.2 us)
Async XLA Ops:
  88.8 28.9 %copy-start.2 = (f32[2,8192]{1,0:T(2,128)S(1)}, f32[2,8192]{1,0:T(2,128)}, u32[]{:S(2)}) copy-start(f32[2,8192]{1,0:T(2,128)} %param.22) | copy-start | bytes 196612
  88.8 28.9 %copy-start.7 = (f32[8]{0:T(128)S(1)}, f32[8]{0:T(128)}, u32[]{:S(2)}) copy-start(f32[8]{0:T(128)} %param.23) | copy-start | bytes 100
  110.5 532.2 %all-to-all-start = ((f32[32,3,1024]{2,1,0:T(4,128)}), f32[32,3,1024]{2,1,0:T(4,128)}, u32[]{:S(2)}, u32[]{:S(2)}) async-start(f32[32,3,1024]{2,1,0:T(4,128)} %copy.248), calls=%async_computation | async-start | bytes 1048576 | tf_op jit(solution)/shard_map/all_to_all | solution.py:125
  117.9 10.6 %copy-start.5 = (s32[2,512]{1,0:T(2,128)S(1)}, s32[2,512]{1,0:T(2,128)}, u32[]{:S(2)}) copy-start(s32[2,512]{1,0:T(2,128)} %param.25) | copy-start | bytes 12292
  117.9 30.9 %copy-start.1 = (f32[16384]{0:T(1024)S(1)}, f32[16384]{0:T(1024)}, u32[]{:S(2)}) copy-start(f32[16384]{0:T(1024)} %param.20) | copy-start | bytes 196612
  117.9 39.8 %copy-start = (s32[6,8192]{1,0:T(8,128)S(1)}, s32[6,8192]{1,0:T(8,128)}, u32[]{:S(2)}) copy-start(s32[6,8192]{1,0:T(8,128)} %param.24) | copy-start | bytes 589828
  117.9 39.8 %copy-start.3 = (f32[8192]{0:T(1024)S(1)}, f32[8192]{0:T(1024)}, u32[]{:S(2)}) copy-start(f32[8192]{0:T(1024)} %param.26) | copy-start | bytes 98308
  136.1 21.6 %collective-permute-start.1 = (f32[3,8,1,512]{3,1,2,0:T(8,128)S(1)}, f32[3,8,1,512]{3,1,2,0:T(8,128)S(1)}, u32[]{:S(2)}, u32[]{:S(2)}) collective-permute-start(f32[3,8,1,512]{3,1,2,0:T(8,128)S(1)} %copy.243), channel_id=1, source_target_pairs={{1,0},{2,1},{3,2},{4,3},{5,4},{6,5},{7,6},{8,7},{9,8},{10,9},{11,1... | collective-permute-start | bytes 147464 | tf_op jit(solution)/shard_map/ppermute | solution.py:19
  148.7 8.9 %collective-permute-start = (f32[3,8,1,512]{3,1,2,0:T(8,128)S(1)}, f32[3,8,1,512]{3,1,2,0:T(8,128)S(1)}, u32[]{:S(2)}, u32[]{:S(2)}) collective-permute-start(f32[3,8,1,512]{3,1,2,0:T(8,128)S(1)} %copy.241), channel_id=1, source_target_pairs={{0,1},{1,2},{2,3},{3,4},{4,5},{5,6},{6,7},{7,8},{8,9},{9,10},{10,1... | collective-permute-start | bytes 147464 | tf_op jit(solution)/shard_map/ppermute | solution.py:18
  651.9 114.7 %copy-start.6 = (f32[1,3]{1,0:T(1,128)S(1)}, f32[1,3]{1,0:T(1,128)}, u32[]{:S(2)}) copy-start(f32[1,3]{1,0:T(1,128)} %param.21) | copy-start | bytes 40
